TPU v7x, 32 devices: a whole 2x2x4 slice. The times are simulated.
32 devices in a mesh: groups: 2 (over x), slab: 16 (over z, y, core).
Axes of the slice: x: 2, y: 2, z: 4, core: 2. Of those that a mesh axis runs over, the one named last changes fastest.
Arguments:
- latent: bfloat16 [64, 32, 2048], P(None, ('groups', 'slab')), parts along dimension 1, may hold values from -6 to 6
- conv1_weight: bfloat16 [27, 64, 64], replicated, may hold values from -0.15625 to 0.15625
- conv2_weight: bfloat16 [27, 64, 64], replicated, may hold values from -0.15625 to 0.15625
- head: bfloat16 [64], replicated, may hold values from -2 to 2
- p_prev: float32 [32, 16, 64, 128], P(('groups', 'slab')), parts along dimension 0, may hold values from -6 to 6
- p_cur: float32 [32, 16, 64, 128], P(('groups', 'slab')), parts along dimension 0, may hold values from -6 to 6
- adjoint: bfloat16 [4, 32, 16, 64, 128], P(None, ('groups', 'slab')), parts along dimension 1, may hold values from -6 to 6
- wavelet: float32 [16, 4], P('groups'), parts along dimension 0, may hold values from -12 to 12
- sources: int32 [16, 3], P('groups'), parts along dimension 0, may hold values from 0 to 127, as said below
- receivers: int32 [16, 3, 128], P('groups'), parts along dimension 0, may hold values from 0 to 127, as said below
Outputs:
- pressure_final: float32 [32, 16, 64, 128], P(('groups', 'slab')), parts along dimension 0
- traces: float32 [16, 4, 128], P('groups'), parts along dimension 0
- gradient: float32 [32, 2048], P(('groups', 'slab')), parts along dimension 0
There are 2 independent parts, one for each index of `groups`. A program takes and returns all parts, laid end to end along the dimension named above; an argument that names none is the same for every part. Nothing has to cross between parts.
Inputs may be any that keep to these rules, and one draw needn't show every extreme that they name: sources[s] is the source cell (depth, row, column) of shot s on the fine grid: depth below 32, row below 64, column below 128. receivers[s, :, k] is the cell (depth, row, column) of receiver k of shot s on the fine grid: depth below 32, row below 64, column below 128.
All inputs are finite; a program needn't handle non-finite values.
Results may differ from a plain program's by a relative error of at most 0.006.
Values may be sent and summed in bfloat16 or wider, within the bound.
A program may use at most 64 MiB of HBM per device.

v0:
```python
import jax
import jax.numpy as jnp
from jax import lax
from jax.sharding import PartitionSpec as P

CY = 32
CX = 64
SHOTS = 8
STEPS = 4
stencil_weights = (-205.0 / 72.0, 8.0 / 5.0, -1.0 / 5.0, 8.0 / 315.0, -1.0 / 560.0)
lowest_speed = 1.5
speed_range = 3.0
courant = 0.088
leak_slope = 0.2


def extended_2(block, sides, width):
    for axis, dim in sides:
        count = lax.axis_size(axis)
        forward = [(i, i + 1) for i in range(count - 1)]
        backward = [(target, source) for source, target in forward]
        low = lax.ppermute(
            lax.slice_in_dim(block, block.shape[dim] - width, None, axis=dim), axis, forward
        )
        high = lax.ppermute(lax.slice_in_dim(block, 0, width, axis=dim), axis, backward)
        block = jnp.concatenate([low, block, high], axis=dim)
    return block


def from_partner(value, axis, apart):
    mask = 2**apart
    pairs = [(source, source ^ mask) for source in range(lax.axis_size(axis))]
    return lax.ppermute(value, axis, pairs)


def for_sending(shard):
    return jax.tree.map(lambda a: a.astype(jnp.bfloat16) if a.dtype == jnp.float32 else a, shard)


def from_behind(value, axis, steps):
    count = lax.axis_size(axis)
    leading, last = (max(0, -steps), min(count, count - steps))
    return lax.ppermute(value, axis, [(source, source + steps) for source in range(leading, last)])


def conv_taps(extended_in, weight):
    planes = extended_in.shape[1] - 2
    cell_count = extended_in.shape[2]
    extended = jnp.pad(extended_in, ((0, 0), (0, 0), (CX + 1, CX + 1)))
    columns = jnp.arange(cell_count) % CX
    accumulated = jnp.zeros((weight.shape[1], planes, cell_count), jnp.float32)
    tap_index = 0
    for depth_off in range(3):
        for row_off in (-1, 0, 1):
            for col_off in (-1, 0, 1):
                begin_at = CX + 1 + row_off * CX + col_off
                piece = extended[
                    :, depth_off : depth_off + planes, begin_at : begin_at + cell_count
                ]
                column_valid = ((columns + col_off >= 0) & (columns + col_off < CX)).astype(
                    extended.dtype
                )
                accumulated = accumulated + jnp.einsum(
                    "oi,izn->ozn",
                    weight[tap_index],
                    piece * column_valid,
                    preferred_element_type=jnp.float32,
                )
                tap_index += 1
    return accumulated


def double_axis(values, axis):
    length = values.shape[axis]
    lower_side = jnp.concatenate(
        [
            lax.slice_in_dim(values, 0, 1, axis=axis),
            lax.slice_in_dim(values, 0, length - 1, axis=axis),
        ],
        axis=axis,
    )
    upper_side = jnp.concatenate(
        [
            lax.slice_in_dim(values, 1, length, axis=axis),
            lax.slice_in_dim(values, length - 1, length, axis=axis),
        ],
        axis=axis,
    )
    even_part = 0.75 * values + 0.25 * lower_side
    odd_part = 0.75 * values + 0.25 * upper_side
    new_shape = list(values.shape)
    new_shape[axis] = 2 * length
    return jnp.stack([even_part, odd_part], axis=axis + 1).reshape(new_shape)


def double_depth(rimmed):
    inner_planes = rimmed.shape[0] - 2
    middle = rimmed[1:-1]
    even_part = 0.75 * middle + 0.25 * rimmed[:-2]
    odd_part = 0.75 * middle + 0.25 * rimmed[2:]
    return jnp.stack([even_part, odd_part], axis=1).reshape((2 * inner_planes,) + rimmed.shape[1:])


def upsample_slab(rimmed):
    deeper = double_depth(rimmed).reshape(2 * (rimmed.shape[0] - 2), CY, CX)
    return double_axis(double_axis(deeper, 1), 2)


def stencil(extended):
    depth_total = extended.shape[0] - 8
    row_total = extended.shape[1]
    col_total = extended.shape[2]
    padded = jnp.pad(extended, ((0, 0), (4, 4), (4, 4)))

    def window(depth_at, row_at, col_at):
        return padded[
            depth_at : depth_at + depth_total,
            row_at : row_at + row_total,
            col_at : col_at + col_total,
        ]

    accumulated = 3.0 * stencil_weights[0] * window(4, 4, 4)
    for reach in range(1, 5):
        near_sum = window(4 - reach, 4, 4) + window(4 + reach, 4, 4)
        near_sum = near_sum + window(4, 4 - reach, 4) + window(4, 4 + reach, 4)
        near_sum = near_sum + window(4, 4, 4 - reach) + window(4, 4, 4 + reach)
        accumulated = accumulated + stencil_weights[reach] * near_sum
    return accumulated


def body(
    latent, conv1_weight, conv2_weight, head, p_prev, p_cur, adjoint, wavelet, sources, receivers
):
    position = lax.axis_index("slab")
    devices = lax.axis_size("slab")
    my_shot = position % SHOTS
    slab_index = position // SHOTS
    slab_total = devices // SHOTS
    group_bits = SHOTS.bit_length() - 1
    latent_wide = extended_2(latent, (("slab", 1),), 1)
    hidden = jax.nn.leaky_relu(conv_taps(latent_wide, conv1_weight), leak_slope).astype(
        jnp.bfloat16
    )
    hidden_wide = extended_2(hidden, (("slab", 1),), 1)
    second = jax.nn.leaky_relu(conv_taps(hidden_wide, conv2_weight), leak_slope)
    logits = jnp.einsum(
        "c,czn->zn", head.astype(jnp.float32), second, precision=lax.Precision.HIGHEST
    )
    velocity = (lowest_speed + speed_range * jax.nn.sigmoid(logits)).astype(jnp.bfloat16)
    planes = velocity.shape[0]
    slab_planes = planes * SHOTS
    rimmed = extended_2(velocity, (("slab", 0),), 1)
    rimmed = jnp.concatenate(
        [
            jnp.where(position == 0, velocity, rimmed[:1]),
            rimmed[1:-1],
            jnp.where(position == devices - 1, velocity, rimmed[-1:]),
        ],
        axis=0,
    )
    tile_doubled = double_depth(rimmed.astype(jnp.float32))
    bit_order = list(range(group_bits))
    blocks = tile_doubled[None]
    for bit_index in bit_order:
        partner = from_partner(blocks, "slab", bit_index)
        upper_bit = my_shot // (1 << bit_index) % 2 == 1
        blocks = jnp.where(
            upper_bit,
            jnp.concatenate([partner, blocks], axis=0),
            jnp.concatenate([blocks, partner], axis=0),
        )
    placed = []
    for shot_number in range(SHOTS):
        list_index = 0
        for section_number in range(group_bits):
            list_index = list_index + (
                (shot_number >> bit_order[section_number] & 1) << section_number
            )
        placed.append(blocks[list_index])
    deeper = jnp.concatenate(placed, axis=0).reshape(2 * slab_planes, CY, CX)
    fine_speed = double_axis(double_axis(deeper, 1), 2)
    courant_sq = (courant * fine_speed) ** 2
    previous = p_prev[0]
    current = p_cur[0]
    fine_planes = current.shape[0]
    offset = slab_index * fine_planes
    source = lax.dynamic_index_in_dim(sources, my_shot, 0, keepdims=False)
    station = lax.dynamic_index_in_dim(receivers, my_shot, 0, keepdims=False)
    pulses = lax.dynamic_index_in_dim(wavelet, my_shot, 0, keepdims=False)
    source_depth = source[0] - offset
    source_inside = (source_depth >= 0) & (source_depth < fine_planes)
    source_depth = jnp.clip(source_depth, 0, fine_planes - 1)
    station_depth = station[0] - offset
    station_inside = (station_depth >= 0) & (station_depth < fine_planes)
    station_depth = jnp.clip(station_depth, 0, fine_planes - 1)
    correlation = jnp.zeros(current.shape, jnp.float32)
    samples_list = []
    for step_index in range(STEPS):
        rim_below = from_behind(for_sending(current[-4:]), "slab", SHOTS)
        rim_above = from_behind(for_sending(current[:4]), "slab", -SHOTS)
        laplace_term = stencil(jnp.concatenate([rim_below, current, rim_above], axis=0))
        correlation = correlation + adjoint[step_index, 0].astype(jnp.float32) * laplace_term
        advanced = 2.0 * current - previous + courant_sq * laplace_term
        advanced = advanced.at[source_depth, source[1], source[2]].add(
            jnp.where(source_inside, pulses[step_index], 0.0)
        )
        samples_list.append(
            jnp.where(station_inside, advanced[station_depth, station[1], station[2]], 0.0)
        )
        previous, current = (current, advanced)
    record = jnp.stack(samples_list)
    own_traces = jnp.where((jnp.arange(SHOTS) == my_shot)[:, None, None], record[None], 0.0)
    traces = lax.psum(own_traces, "slab")
    fine_gradient = 2.0 * courant * courant * fine_speed * correlation
    shape_holder = jnp.zeros((slab_planes + 2, velocity.shape[1]), jnp.float32)
    unused, pullback = jax.vjp(upsample_slab, shape_holder)
    grad_rim = pullback(fine_gradient)[0]
    first_slab = slab_index == 0
    last_slab = slab_index == slab_total - 1
    folded = jnp.concatenate(
        [
            jnp.where(first_slab, 0.0, grad_rim[:1]),
            grad_rim[1:2] + jnp.where(first_slab, grad_rim[:1], 0.0),
            grad_rim[2:-2],
            grad_rim[-2:-1] + jnp.where(last_slab, grad_rim[-1:], 0.0),
            jnp.where(last_slab, 0.0, grad_rim[-1:]),
        ],
        axis=0,
    )
    from_lower = from_behind(folded[-1:], "slab", SHOTS)
    from_upper = from_behind(folded[:1], "slab", -SHOTS)
    inner = folded[1:-1]
    inner = jnp.concatenate([inner[:1] + from_lower, inner[1:-1], inner[-1:] + from_upper], axis=0)
    blocks = inner.reshape(SHOTS, planes, inner.shape[1])
    for bit_index in reversed(range(group_bits)):
        halfway = blocks.shape[0] // 2
        upper_bit = my_shot // (1 << bit_index) % 2 == 1
        retained = jnp.where(upper_bit, blocks[halfway:], blocks[:halfway])
        outgoing = jnp.where(upper_bit, blocks[:halfway], blocks[halfway:])
        blocks = retained + from_partner(outgoing, "slab", bit_index)
    gradient = blocks[0]
    return (current[None], traces, gradient)


def solution(mesh):
    in_specs = (
        P(None, ("groups", "slab"), None),
        P(),
        P(),
        P(),
        P(("groups", "slab"), None, None, None),
        P(("groups", "slab"), None, None, None),
        P(None, ("groups", "slab"), None, None, None),
        P("groups", None),
        P("groups", None),
        P("groups", None, None),
    )
    out_specs = (
        P(("groups", "slab"), None, None, None),
        P("groups", None, None),
        P(("groups", "slab"), None),
    )
    return jax.shard_map(body, mesh=mesh, in_specs=in_specs, out_specs=out_specs, check_vma=False)
```

profile of v0, /device:TPU:0, one launch (start us, length us, event | category | flops | bytes accessed | tf_op | source)
XLA Modules:
  0.0 228.8 jit_solution(11264955654170186735)
XLA Ops:
  2.1 3.1 %collective-permute-start = (bf16[64,1,2048]{2,0,1:T(8,128)(2,1)}, bf16[64,1,2048]{2,0,1:T(8,128)(2,1)S(1)}, u32[]{:S(2)}, u32[]{:S(2)}) collective-permute-start(bf16[64,1,2048]{2,0,1:T(8,128)(2,1)} %param.18), channel_id=1, source_target_pairs={{0,1},{1,2},{2,3},{3,4},{4,5},{5,6},{6,7},{7,8},{8,9},{9,10},{10,1... | collective-permute-start | bytes 786440 | tf_op jit(solution)/shard_map/ppermute | solution.py:22
  16.5 9.2 %collective-permute-start.2 = (bf16[64,1,2048]{2,0,1:T(8,128)(2,1)S(1)}, bf16[64,1,2048]{2,0,1:T(8,128)(2,1)S(1)}, u32[]{:S(2)}, u32[]{:S(2)}) collective-permute-start(bf16[64,1,2048]{2,0,1:T(8,128)(2,1)S(1)} %bitcast.577), channel_id=1, source_target_pairs={{0,1},{1,2},{2,3},{3,4},{4,5},{5,6},{6,7},{7,8},{8,9},{9,10},{10,1... | collective-permute-start | bytes 786440 | tf_op jit(solution)/shard_map/ppermute | solution.py:22
  25.7 5.7 %collective-permute-start.9 = (bf16[4,64,128]{2,1,0:T(8,128)(2,1)S(1)}, bf16[4,64,128]{2,1,0:T(8,128)(2,1)S(1)}, u32[]{:S(2)}, u32[]{:S(2)}) collective-permute-start(bf16[4,64,128]{2,1,0:T(8,128)(2,1)S(1)} %get-tuple-element.81), channel_id=1, source_target_pairs={{0,8},{1,9},{2,10},{3,11},{4,12},{5,13},{6,14},{7,15},{16,24},{17,... | collective-permute-start | bytes 196616 | tf_op jit(solution)/shard_map/ppermute | solution.py:43
  42.9 3.6 %collective-permute-start.4 = (bf16[1,2048]{1,0:T(2,128)(2,1)S(1)}, bf16[1,2048]{1,0:T(2,128)(2,1)S(1)}, u32[]{:S(2)}, u32[]{:S(2)}) collective-permute-start(bf16[1,2048]{1,0:T(2,128)(2,1)S(1)} %convert_element_type.266), channel_id=1, source_target_pairs={{0,1},{1,2},{2,3},{3,4},{4,5},{5,6},{6,7},{7,8},{8,9},{9,10},{10,1... | collective-permute-start | bytes 12296 | tf_op jit(solution)/shard_map/ppermute | solution.py:22
  47.4 1.8 collective-permute-start.6
  54.2 2.4 %collective-permute-start.7 = (f32[2,2,2048]{2,1,0:T(2,128)S(1)}, f32[2,2,2048]{2,1,0:T(2,128)S(1)}, u32[]{:S(2)}, u32[]{:S(2)}) collective-permute-start(f32[2,2,2048]{2,1,0:T(2,128)S(1)} %maximum_select_fusion.2), channel_id=1, source_target_pairs={{0,2},{1,3},{2,0},{3,1},{4,6},{5,7},{6,4},{7,5},{8,10},{9,11},{10,... | collective-permute-start | bytes 98312 | tf_op jit(solution)/shard_map/ppermute | solution.py:33
  60.1 2.2 collective-permute-start.8
  62.8 1.7 collective-permute-done.8
  72.2 1.7 fusion.155
  75.1 1.9 copy.58
  77.0 1.6 copy.59
  78.6 4.4 %fusion.164 = (f32[16,64,128]{2,1,0:T(8,128)S(1)}, f32[16,64,128]{2,1,0:T(8,128)}) fusion(f32[1,16,64,128]{3,2,1,0:T(8,128)} %param.22, f32[16,64,128]{2,1,0:T(8,128)S(1)} %copy.59, f32[1,16,64,128]{3,2,1,0:T(8,128)S(1)} %copy-done.2, f32[24,72,136]{2,1,0:T(8,128)S(1)} %select_maximum_fusion.6, f32[4,64,128]{2,1,0:T(8,128)} %copy-done.11, ...), kind=kLoop, calls=%fused_computation.321 | loop fusion | flops 5373952 | bytes 11796480 | tf_op jit(solution)/shard_map/add | solution.py:203
  85.7 5.2 %collective-permute-start.11 = (bf16[4,64,128]{2,1,0:T(8,128)(2,1)S(1)}, bf16[4,64,128]{2,1,0:T(8,128)(2,1)S(1)}, u32[]{:S(2)}, u32[]{:S(2)}) collective-permute-start(bf16[4,64,128]{2,1,0:T(8,128)(2,1)S(1)} %get-tuple-element.79), channel_id=1, source_target_pairs={{0,8},{1,9},{2,10},{3,11},{4,12},{5,13},{6,14},{7,15},{16,24},{17,... | collective-permute-start | bytes 196616 | tf_op jit(solution)/shard_map/ppermute | solution.py:43
  92.7 5.2 %collective-permute-done.12 = bf16[4,64,128]{2,1,0:T(8,128)(2,1)S(1)} collective-permute-done((bf16[4,64,128]{2,1,0:T(8,128)(2,1)S(1)}, bf16[4,64,128]{2,1,0:T(8,128)(2,1)S(1)}, u32[]{:S(2)}, u32[]{:S(2)}) %collective-permute-start.12) | collective-permute-done | bytes 65568 | tf_op jit(solution)/shard_map/ppermute | solution.py:43
  99.1 4.2 %multiply_add_fusion.2 = (f32[16,64,128]{2,1,0:T(8,128)S(1)}, f32[16,64,128]{2,1,0:T(8,128)}) fusion(f32[16,64,128]{2,1,0:T(8,128)} %copy-done.3, f32[16,64,128]{2,1,0:T(8,128)S(1)} %scatter-add.14, f32[1,16,64,128]{3,2,1,0:T(8,128)S(1)} %copy-done.2, f32[24,72,136]{2,1,0:T(8,128)S(1)} %select_maximum_fusion.4, f32[4,64,128]{2,1,0:T(8,128)} %copy-done.13, ...), kind=kLoop, calls=%fused_computation.326 | loop fusion | flops 5373952 | bytes 11272192 | tf_op jit(solution)/shard_map/add | solution.py:203
  106.1 1.6 collective-permute-start.13
  107.7 1.5 collective-permute-start.14
  110.0 1.5 gather_fusion
  111.5 3.3 %collective-permute-done.14 = bf16[4,64,128]{2,1,0:T(8,128)(2,1)S(1)} collective-permute-done((bf16[4,64,128]{2,1,0:T(8,128)(2,1)S(1)}, bf16[4,64,128]{2,1,0:T(8,128)(2,1)S(1)}, u32[]{:S(2)}, u32[]{:S(2)}) %collective-permute-start.14) | collective-permute-done | bytes 65568 | tf_op jit(solution)/shard_map/ppermute | solution.py:43
  116.0 4.2 %multiply_add_fusion.1 = (f32[16,64,128]{2,1,0:T(8,128)S(1)}, f32[16,64,128]{2,1,0:T(8,128)}) fusion(f32[16,64,128]{2,1,0:T(8,128)} %copy-done.3, f32[16,64,128]{2,1,0:T(8,128)S(1)} %scatter-add.14, f32[16,64,128]{2,1,0:T(8,128)S(1)} %scatter-add.15, f32[24,72,136]{2,1,0:T(8,128)S(1)} %select_maximum_fusion.2, f32[4,64,128]{2,1,0:T(8,128)} %copy-done.12, ...), kind=kLoop, calls=%fused_computation.325 | loop fusion | flops 5373952 | bytes 11272192 | tf_op jit(solution)/shard_map/add | solution.py:203
  123.0 2.2 collective-permute-start.15
  127.2 2.0 copy.63
  129.2 2.4 %copy.64 = f32[16,64,128]{2,1,0:T(8,128)} copy(f32[16,64,128]{1,0,2:T(8,128)} %bitcast.569) | data formatting | bytes 1048576 | tf_op jit(solution)/shard_map/mul | solution.py:214
  136.0 3.4 %fusion.158 = (f32[16,64,128]{2,1,0:T(8,128)}, f32[16,64,128]{2,1,0:T(8,128)S(1)}) fusion(f32[16,64,128]{2,1,0:T(8,128)S(1)} %copy-done.10, f32[16,64,128]{2,1,0:T(8,128)S(1)} %copy-done.9, f32[16,64,128]{2,1,0:T(8,128)S(1)} %copy-done.8, f32[16,64,128]{2,1,0:T(8,128)S(1)} %copy-done.7, bf16[4,1,16,64,128]{4,3,2,1,0:T(8,128)(2,1)S(1)} %copy-done.14, ...), kind=kLoop, calls=%fused_computation.310 | loop fusion | flops 6422528 | bytes 13369344 | tf_op jit(solution)/shard_map/mul | solution.py:214
  143.7 1.5 copy.65
  148.5 5.4 %collective-permute-start.18 = (f32[1,2048]{1,0:T(1,128)S(1)}, f32[1,2048]{1,0:T(1,128)S(1)}, u32[]{:S(2)}, u32[]{:S(2)}) collective-permute-start(f32[1,2048]{1,0:T(1,128)S(1)} %get-tuple-element.91), channel_id=1, source_target_pairs={{0,8},{1,9},{2,10},{3,11},{4,12},{5,13},{6,14},{7,15},{16,24},{17,... | collective-permute-start | bytes 24584 | tf_op jit(solution)/shard_map/ppermute | solution.py:43
  155.3 5.1 %collective-permute-done.17 = f32[1,2048]{1,0:T(1,128)S(1)} collective-permute-done((f32[1,2048]{1,0:T(1,128)S(1)}, f32[1,2048]{1,0:T(1,128)S(1)}, u32[]{:S(2)}, u32[]{:S(2)}) %collective-permute-start.17) | collective-permute-done | bytes 8224 | tf_op jit(solution)/shard_map/ppermute | solution.py:43
  160.5 2.1 collective-permute-start.19
  162.6 1.9 collective-permute-done.19
  164.5 1.8 collective-permute-start.20
  166.4 2.0 collective-permute-done.20
  168.4 59.7 %psum.7 = f32[8,4,128]{2,1,0:T(4,128)} all-reduce(f32[8,4,128]{2,1,0:T(4,128)S(1)} %broadcast_select_fusion.9), channel_id=1, replica_groups=mesh['groups'=2,'slab'=16] {'slab'}, use_global_device_ids=true, to_apply=%region_1.2 | all-reduce | flops 4096 | bytes 32768 | tf_op jit(solution)/shard_map/psum | solution.py:213
  (255 shorter events, 56.6 us)
Async XLA Ops:
  0.6 32.1 %copy-start = (f32[8,4]{0,1:T(4,128)S(1)}, f32[8,4]{0,1:T(4,128)}, u32[]{:S(2)}) copy-start(f32[8,4]{0,1:T(4,128)} %param.25) | copy-start | bytes 388
  0.6 7.1 %copy-start.17 = (bf16[27,64,64]{2,1,0:T(8,128)(2,1)S(1)}, bf16[27,64,64]{2,1,0:T(8,128)(2,1)}, u32[]{:S(2)}) copy-start(bf16[27,64,64]{2,1,0:T(8,128)(2,1)} %param.19) | copy-start | bytes 663556
  0.7 5.6 %collective-permute-start.1 = (bf16[64,1,2048]{2,0,1:T(8,128)(2,1)}, bf16[64,1,2048]{2,0,1:T(8,128)(2,1)S(1)}, u32[]{:S(2)}, u32[]{:S(2)}) collective-permute-start(bf16[64,1,2048]{2,0,1:T(8,128)(2,1)} %param.18), channel_id=1, source_target_pairs={{1,0},{2,1},{3,2},{4,3},{5,4},{6,5},{7,6},{8,7},{9,8},{10,9},{11,1... | collective-permute-start | bytes 786440 | tf_op jit(solution)/shard_map/ppermute | solution.py:25
  2.1 4.4 %collective-permute-start = (bf16[64,1,2048]{2,0,1:T(8,128)(2,1)}, bf16[64,1,2048]{2,0,1:T(8,128)(2,1)S(1)}, u32[]{:S(2)}, u32[]{:S(2)}) collective-permute-start(bf16[64,1,2048]{2,0,1:T(8,128)(2,1)} %param.18), channel_id=1, source_target_pairs={{0,1},{1,2},{2,3},{3,4},{4,5},{5,6},{6,7},{7,8},{8,9},{9,10},{10,1... | collective-permute-start | bytes 786440 | tf_op jit(solution)/shard_map/ppermute | solution.py:22
  14.9 19.0 %copy-start.16 = (bf16[27,64,64]{2,1,0:T(8,128)(2,1)S(1)}, bf16[27,64,64]{2,1,0:T(8,128)(2,1)}, u32[]{:S(2)}) copy-start(bf16[27,64,64]{2,1,0:T(8,128)(2,1)} %param.20) | copy-start | bytes 663556
  15.2 18.2 %collective-permute-start.3 = (bf16[64,1,2048]{2,0,1:T(8,128)(2,1)S(1)}, bf16[64,1,2048]{2,0,1:T(8,128)(2,1)S(1)}, u32[]{:S(2)}, u32[]{:S(2)}) collective-permute-start(bf16[64,1,2048]{2,0,1:T(8,128)(2,1)S(1)} %bitcast.576), channel_id=1, source_target_pairs={{1,0},{2,1},{3,2},{4,3},{5,4},{6,5},{7,6},{8,7},{9,8},{10,9},{11,1... | collective-permute-start | bytes 786440 | tf_op jit(solution)/shard_map/ppermute | solution.py:25
  16.5 16.9 %collective-permute-start.2 = (bf16[64,1,2048]{2,0,1:T(8,128)(2,1)S(1)}, bf16[64,1,2048]{2,0,1:T(8,128)(2,1)S(1)}, u32[]{:S(2)}, u32[]{:S(2)}) collective-permute-start(bf16[64,1,2048]{2,0,1:T(8,128)(2,1)S(1)} %bitcast.577), channel_id=1, source_target_pairs={{0,1},{1,2},{2,3},{3,4},{4,5},{5,6},{6,7},{7,8},{8,9},{9,10},{10,1... | collective-permute-start | bytes 786440 | tf_op jit(solution)/shard_map/ppermute | solution.py:22
  25.7 34.2 %collective-permute-start.9 = (bf16[4,64,128]{2,1,0:T(8,128)(2,1)S(1)}, bf16[4,64,128]{2,1,0:T(8,128)(2,1)S(1)}, u32[]{:S(2)}, u32[]{:S(2)}) collective-permute-start(bf16[4,64,128]{2,1,0:T(8,128)(2,1)S(1)} %get-tuple-element.81), channel_id=1, source_target_pairs={{0,8},{1,9},{2,10},{3,11},{4,12},{5,13},{6,14},{7,15},{16,24},{17,... | collective-permute-start | bytes 196616 | tf_op jit(solution)/shard_map/ppermute | solution.py:43
  31.4 28.6 %collective-permute-start.10 = (bf16[4,64,128]{2,1,0:T(8,128)(2,1)S(1)}, bf16[4,64,128]{2,1,0:T(8,128)(2,1)S(1)}, u32[]{:S(2)}, u32[]{:S(2)}) collective-permute-start(bf16[4,64,128]{2,1,0:T(8,128)(2,1)S(1)} %get-tuple-element.82), channel_id=1, source_target_pairs={{8,0},{9,1},{10,2},{11,3},{12,4},{13,5},{14,6},{15,7},{24,16},{25,... | collective-permute-start | bytes 196616 | tf_op jit(solution)/shard_map/ppermute | solution.py:43
  40.7 5.9 %copy-start.18 = (s32[8,3]{0,1:T(4,128)S(1)}, s32[8,3]{0,1:T(4,128)}, u32[]{:S(2)}) copy-start(s32[8,3]{0,1:T(4,128)} %param.26) | copy-start | bytes 292
  40.7 16.0 %copy-start.21 = (s32[3]{0:T(128)S(1)}, s32[3]{0:T(128)}, u32[]{:S(2)}) copy-start(s32[3]{0:T(128)} %constant.246.clone.1) | copy-start | bytes 40
  40.7 21.6 %copy-start.2 = (f32[1,16,64,128]{3,2,1,0:T(8,128)S(1)}, f32[1,16,64,128]{3,2,1,0:T(8,128)}, u32[]{:S(2)}) copy-start(f32[1,16,64,128]{3,2,1,0:T(8,128)} %param.23) | copy-start | bytes 1572868
  41.6 5.0 %collective-permute-start.5 = (bf16[1,2048]{1,0:T(2,128)(2,1)S(1)}, bf16[1,2048]{1,0:T(2,128)(2,1)S(1)}, u32[]{:S(2)}, u32[]{:S(2)}) collective-permute-start(bf16[1,2048]{1,0:T(2,128)(2,1)S(1)} %convert_element_type.266), channel_id=1, source_target_pairs={{1,0},{2,1},{3,2},{4,3},{5,4},{6,5},{7,6},{8,7},{9,8},{10,9},{11,1... | collective-permute-start | bytes 12296 | tf_op jit(solution)/shard_map/ppermute | solution.py:25
  42.9 4.3 %collective-permute-start.4 = (bf16[1,2048]{1,0:T(2,128)(2,1)S(1)}, bf16[1,2048]{1,0:T(2,128)(2,1)S(1)}, u32[]{:S(2)}, u32[]{:S(2)}) collective-permute-start(bf16[1,2048]{1,0:T(2,128)(2,1)S(1)} %convert_element_type.266), channel_id=1, source_target_pairs={{0,1},{1,2},{2,3},{3,4},{4,5},{5,6},{6,7},{7,8},{8,9},{9,10},{10,1... | collective-permute-start | bytes 12296 | tf_op jit(solution)/shard_map/ppermute | solution.py:22
  47.4 6.8 %collective-permute-start.6 = (f32[1,2,2048]{2,1,0:T(2,128)S(1)}, f32[1,2,2048]{2,1,0:T(2,128)S(1)}, u32[]{:S(2)}, u32[]{:S(2)}) collective-permute-start(f32[1,2,2048]{2,1,0:T(2,128)S(1)} %pad_maximum_fusion.12), channel_id=1, source_target_pairs={{0,1},{1,0},{2,3},{3,2},{4,5},{5,4},{6,7},{7,6},{8,9},{9,8},{10,11... | collective-permute-start | bytes 49160 | tf_op jit(solution)/shard_map/ppermute | solution.py:33
  54.2 5.8 %collective-permute-start.7 = (f32[2,2,2048]{2,1,0:T(2,128)S(1)}, f32[2,2,2048]{2,1,0:T(2,128)S(1)}, u32[]{:S(2)}, u32[]{:S(2)}) collective-permute-start(f32[2,2,2048]{2,1,0:T(2,128)S(1)} %maximum_select_fusion.2), channel_id=1, source_target_pairs={{0,2},{1,3},{2,0},{3,1},{4,6},{5,7},{6,4},{7,5},{8,10},{9,11},{10,... | collective-permute-start | bytes 98312 | tf_op jit(solution)/shard_map/ppermute | solution.py:33
  60.0 5.3 %copy-start.11 = (f32[4,64,128]{2,1,0:T(8,128)}, f32[4,64,128]{2,1,0:T(8,128)S(1)}, u32[]{:S(2)}) copy-start(f32[4,64,128]{2,1,0:T(8,128)S(1)} %convert_element_type.271) | copy-start | bytes 393220
  60.1 4.5 %collective-permute-start.8 = (f32[4,2,2048]{2,1,0:T(2,128)S(1)}, f32[4,2,2048]{2,1,0:T(2,128)S(1)}, u32[]{:S(2)}, u32[]{:S(2)}) collective-permute-start(f32[4,2,2048]{2,1,0:T(2,128)S(1)} %maximum_select_fusion.1), channel_id=1, source_target_pairs={{0,4},{1,5},{2,6},{3,7},{4,0},{5,1},{6,2},{7,3},{8,12},{9,13},{10,... | collective-permute-start | bytes 196616 | tf_op jit(solution)/shard_map/ppermute | solution.py:33
  78.6 4.4 %copy-start.3 = (f32[16,64,128]{2,1,0:T(8,128)}, f32[16,64,128]{2,1,0:T(8,128)S(1)}, u32[]{:S(2)}) copy-start(f32[16,64,128]{2,1,0:T(8,128)S(1)} %copy.59) | copy-start | bytes 1572868
  85.7 7.1 %collective-permute-start.11 = (bf16[4,64,128]{2,1,0:T(8,128)(2,1)S(1)}, bf16[4,64,128]{2,1,0:T(8,128)(2,1)S(1)}, u32[]{:S(2)}, u32[]{:S(2)}) collective-permute-start(bf16[4,64,128]{2,1,0:T(8,128)(2,1)S(1)} %get-tuple-element.79), channel_id=1, source_target_pairs={{0,8},{1,9},{2,10},{3,11},{4,12},{5,13},{6,14},{7,15},{16,24},{17,... | collective-permute-start | bytes 196616 | tf_op jit(solution)/shard_map/ppermute | solution.py:43
  90.8 7.1 %collective-permute-start.12 = (bf16[4,64,128]{2,1,0:T(8,128)(2,1)S(1)}, bf16[4,64,128]{2,1,0:T(8,128)(2,1)S(1)}, u32[]{:S(2)}, u32[]{:S(2)}) collective-permute-start(bf16[4,64,128]{2,1,0:T(8,128)(2,1)S(1)} %get-tuple-element.80), channel_id=1, source_target_pairs={{8,0},{9,1},{10,2},{11,3},{12,4},{13,5},{14,6},{15,7},{24,16},{25,... | collective-permute-start | bytes 196616 | tf_op jit(solution)/shard_map/ppermute | solution.py:43
  106.1 5.3 %collective-permute-start.13 = (bf16[4,64,128]{2,1,0:T(8,128)(2,1)S(1)}, bf16[4,64,128]{2,1,0:T(8,128)(2,1)S(1)}, u32[]{:S(2)}, u32[]{:S(2)}) collective-permute-start(bf16[4,64,128]{2,1,0:T(8,128)(2,1)S(1)} %get-tuple-element.77), channel_id=1, source_target_pairs={{0,8},{1,9},{2,10},{3,11},{4,12},{5,13},{6,14},{7,15},{16,24},{17,... | collective-permute-start | bytes 196616 | tf_op jit(solution)/shard_map/ppermute | solution.py:43
  107.7 7.1 %collective-permute-start.14 = (bf16[4,64,128]{2,1,0:T(8,128)(2,1)S(1)}, bf16[4,64,128]{2,1,0:T(8,128)(2,1)S(1)}, u32[]{:S(2)}, u32[]{:S(2)}) collective-permute-start(bf16[4,64,128]{2,1,0:T(8,128)(2,1)S(1)} %get-tuple-element.78), channel_id=1, source_target_pairs={{8,0},{9,1},{10,2},{11,3},{12,4},{13,5},{14,6},{15,7},{24,16},{25,... | collective-permute-start | bytes 196616 | tf_op jit(solution)/shard_map/ppermute | solution.py:43
  120.1 7.1 %copy-start.5 = (f32[16,64,64,2]{2,0,1,3:T(8,128)S(1)}, f32[16,64,64,2]{2,0,1,3:T(8,128)}, u32[]{:S(2)}) copy-start(f32[16,64,64,2]{2,0,1,3:T(8,128)} %get-tuple-element.63) | copy-start | bytes 1572868
  123.0 11.6 %collective-permute-start.15 = (bf16[4,64,128]{2,1,0:T(8,128)(2,1)S(1)}, bf16[4,64,128]{2,1,0:T(8,128)(2,1)S(1)}, u32[]{:S(2)}, u32[]{:S(2)}) collective-permute-start(bf16[4,64,128]{2,1,0:T(8,128)(2,1)S(1)} %get-tuple-element.75), channel_id=1, source_target_pairs={{0,8},{1,9},{2,10},{3,11},{4,12},{5,13},{6,14},{7,15},{16,24},{17,... | collective-permute-start | bytes 196616 | tf_op jit(solution)/shard_map/ppermute | solution.py:43
  125.2 9.4 %collective-permute-start.16 = (bf16[4,64,128]{2,1,0:T(8,128)(2,1)S(1)}, bf16[4,64,128]{2,1,0:T(8,128)(2,1)S(1)}, u32[]{:S(2)}, u32[]{:S(2)}) collective-permute-start(bf16[4,64,128]{2,1,0:T(8,128)(2,1)S(1)} %get-tuple-element.76), channel_id=1, source_target_pairs={{8,0},{9,1},{10,2},{11,3},{12,4},{13,5},{14,6},{15,7},{24,16},{25,... | collective-permute-start | bytes 196616 | tf_op jit(solution)/shard_map/ppermute | solution.py:43
  147.4 81.3 %copy-start.1 = (f32[8,4]{0,1:T(4,128)S(1)}, f32[8,4]{0,1:T(4,128)}, u32[]{:S(2)}) copy-start(f32[8,4]{0,1:T(4,128)} %param.25) | copy-start | bytes 388
  148.5 6.8 %collective-permute-start.18 = (f32[1,2048]{1,0:T(1,128)S(1)}, f32[1,2048]{1,0:T(1,128)S(1)}, u32[]{:S(2)}, u32[]{:S(2)}) collective-permute-start(f32[1,2048]{1,0:T(1,128)S(1)} %get-tuple-element.91), channel_id=1, source_target_pairs={{0,8},{1,9},{2,10},{3,11},{4,12},{5,13},{6,14},{7,15},{16,24},{17,... | collective-permute-start | bytes 24584 | tf_op jit(solution)/shard_map/ppermute | solution.py:43
  153.9 6.4 %collective-permute-start.17 = (f32[1,2048]{1,0:T(1,128)S(1)}, f32[1,2048]{1,0:T(1,128)S(1)}, u32[]{:S(2)}, u32[]{:S(2)}) collective-permute-start(f32[1,2048]{1,0:T(1,128)S(1)} %get-tuple-element.92), channel_id=1, source_target_pairs={{8,0},{9,1},{10,2},{11,3},{12,4},{13,5},{14,6},{15,7},{24,16},{25,... | collective-permute-start | bytes 24584 | tf_op jit(solution)/shard_map/ppermute | solution.py:43
  160.5 4.0 %collective-permute-start.19 = (f32[4,1,2048]{2,0,1:T(4,128)S(1)}, f32[4,1,2048]{2,0,1:T(4,128)S(1)}, u32[]{:S(2)}, u32[]{:S(2)}) collective-permute-start(f32[4,1,2048]{2,0,1:T(4,128)S(1)} %select_bitcast_fusion), channel_id=1, source_target_pairs={{0,4},{1,5},{2,6},{3,7},{4,0},{5,1},{6,2},{7,3},{8,12},{9,13},{10,... | collective-permute-start | bytes 98312 | tf_op jit(solution)/shard_map/ppermute | solution.py:33
  164.5 3.8 %collective-permute-start.20 = (f32[2,1,2048]{2,0,1:T(2,128)S(1)}, f32[2,1,2048]{2,0,1:T(2,128)S(1)}, u32[]{:S(2)}, u32[]{:S(2)}) collective-permute-start(f32[2,1,2048]{2,0,1:T(2,128)S(1)} %broadcast_select_fusion.4), channel_id=1, source_target_pairs={{0,2},{1,3},{2,0},{3,1},{4,6},{5,7},{6,4},{7,5},{8,10},{9,11},{10,... | collective-permute-start | bytes 49160 | tf_op jit(solution)/shard_map/ppermute | solution.py:33
  168.3 59.8 %collective-permute-start.21 = (f32[1,1,2048]{2,0,1:T(1,128)S(1)}, f32[1,1,2048]{2,0,1:T(1,128)S(1)}, u32[]{:S(2)}, u32[]{:S(2)}) collective-permute-start(f32[1,1,2048]{2,0,1:T(1,128)S(1)} %broadcast_select_fusion.5), channel_id=1, source_target_pairs={{0,1},{1,0},{2,3},{3,2},{4,5},{5,4},{6,7},{7,6},{8,9},{9,8},{10,11... | collective-permute-start | bytes 24584 | tf_op jit(solution)/shard_map/ppermute | solution.py:33
  (13 other events, 19.8 us)
where the time goes:
time: 230 us; the launch traced here: 229 us
  blocking collectives  59.7 us (26%)
  starting transfers between devices  56.9 us (25%)
  local copies, waits for them, and re-layouts  31.1 us (14%)
  other arithmetic  28.9 us (13%)
  waiting for transfers between devices  20.4 us (9%)
  between operations  16.9 us (7%)
  matrix products  14.7 us (6%)
    psum x1, blocking collectives, body(): traces = lax.psum(own_traces, 'slab')  59.7 us
    ppermute x10, starting transfers between devices, from_behind(): lax.ppermute(value, axis, [(source, source + steps) for source in range(l...  26.7 us
    ppermute x3, starting transfers between devices, extended_2(): lax.ppermute(lax.slice_in_dim(block, block.shape[dim] - width, None, axis...  15.9 us
    dot_general x54, matrix products, conv_taps(): jnp.einsum('oi,izn->ozn', weight[tap_index], piece * column_valid, prefer...  14.4 us
    ppermute x10, waiting for transfers between devices, from_behind(): lax.ppermute(value, axis, [(source, source + steps) for source in range(l...  14.1 us
    add x4, other arithmetic, body(): advanced = 2.0 * current - previous + courant_sq * laplace_term  12.9 us
    ppermute x6, starting transfers between devices, from_partner(): return lax.ppermute(value, axis, pairs)  10.4 us
    gather x4, local copies, waits for them, and re-layouts, body(): advanced[station_depth, station[1], station[2]]  5.93 us
  transfers between devices with their start and end apart: 22, of which 9 were waited for; matrix products, arithmetic and copies ran while one was open for 10% of the time, Pallas kernels for 0%

commit v1 on v0

--- a/solution.py
+++ b/solution.py
@@ -210,7 +210,9 @@
         previous, current = (current, advanced)
     record = jnp.stack(samples_list)
     own_traces = jnp.where((jnp.arange(SHOTS) == my_shot)[:, None, None], record[None], 0.0)
-    traces = lax.psum(own_traces, "slab")
+    traces = own_traces
+    for hop in (1, 2, 4, 8):
+        traces = traces + lax.ppermute(traces, "slab", [(dev, dev ^ hop) for dev in range(16)])
     fine_gradient = 2.0 * courant * courant * fine_speed * correlation
     shape_holder = jnp.zeros((slab_planes + 2, velocity.shape[1]), jnp.float32)
     unused, pullback = jax.vjp(upsample_slab, shape_holder)

time: 230 us -> 175 us (0.76)
  blocking collectives: 59.7 us -> 0 us
  starting transfers between devices: 56.9 us -> 60.3 us
    psum x1 -> x0, blocking collectives: 59.7 us -> none  [body(): traces = lax.psum(own_traces, 'slab')]
    ppermute x0 -> x4, starting transfers between devices: none -> 3.77 us  [body(): lax.ppermute(traces, 'slab', [(dev, dev ^ hop) for dev in range(16)])]
    ppermute x0 -> x4, waiting for transfers between devices: none -> 2.88 us  [body(): lax.ppermute(traces, 'slab', [(dev, dev ^ hop) for dev in range(16)])]
  transfers between devices with their start and end apart: 22 -> 26, of which waited for: 9 -> 11; matrix products, arithmetic and copies ran while one was open for 10% -> 13% of each run, Pallas kernels for 0% -> 0%
where the time goes in v1:
time: 175 us; the launch traced here: 174 us
  starting transfers between devices  60.3 us (34%)
  local copies, waits for them, and re-layouts  31.1 us (18%)
  other arithmetic  29.7 us (17%)
  waiting for transfers between devices  21.4 us (12%)
  between operations  17.2 us (10%)
  matrix products  14.7 us (8%)
    ppermute x10, starting transfers between devices, from_behind(): lax.ppermute(value, axis, [(source, source + steps) for source in range(l...  26.7 us
    ppermute x3, starting transfers between devices, extended_2(): lax.ppermute(lax.slice_in_dim(block, block.shape[dim] - width, None, axis...  15.9 us
    dot_general x54, matrix products, conv_taps(): jnp.einsum('oi,izn->ozn', weight[tap_index], piece * column_valid, prefer...  14.4 us
    ppermute x10, waiting for transfers between devices, from_behind(): lax.ppermute(value, axis, [(source, source + steps) for source in range(l...  14 us
    add x4, other arithmetic, body(): advanced = 2.0 * current - previous + courant_sq * laplace_term  12.9 us
    ppermute x6, starting transfers between devices, from_partner(): return lax.ppermute(value, axis, pairs)  9.89 us
    gather x4, local copies, waits for them, and re-layouts, body(): advanced[station_depth, station[1], station[2]]  5.93 us
    mul x3, local copies, waits for them, and re-layouts, body(): fine_gradient = 2.0 * courant * courant * fine_speed * correlation  5.89 us
  transfers between devices with their start and end apart: 26, of which 11 were waited for; matrix products, arithmetic and copies ran while one was open for 13% of the time, Pallas kernels for 0%

profile of v1, /device:TPU:0, one launch (start us, length us, event | category | flops | bytes accessed | tf_op | source)
XLA Modules:
  0.0 174.3 jit_solution(10183999659742342518)
XLA Ops:
  2.1 3.1 %collective-permute-start = (bf16[64,1,2048]{2,0,1:T(8,128)(2,1)}, bf16[64,1,2048]{2,0,1:T(8,128)(2,1)S(1)}, u32[]{:S(2)}, u32[]{:S(2)}) collective-permute-start(bf16[64,1,2048]{2,0,1:T(8,128)(2,1)} %param.18), channel_id=1, source_target_pairs={{0,1},{1,2},{2,3},{3,4},{4,5},{5,6},{6,7},{7,8},{8,9},{9,10},{10,1... | collective-permute-start | bytes 786440 | tf_op jit(solution)/shard_map/ppermute | solution.py:22
  16.5 9.2 %collective-permute-start.2 = (bf16[64,1,2048]{2,0,1:T(8,128)(2,1)S(1)}, bf16[64,1,2048]{2,0,1:T(8,128)(2,1)S(1)}, u32[]{:S(2)}, u32[]{:S(2)}) collective-permute-start(bf16[64,1,2048]{2,0,1:T(8,128)(2,1)S(1)} %bitcast.577), channel_id=1, source_target_pairs={{0,1},{1,2},{2,3},{3,4},{4,5},{5,6},{6,7},{7,8},{8,9},{9,10},{10,1... | collective-permute-start | bytes 786440 | tf_op jit(solution)/shard_map/ppermute | solution.py:22
  25.7 5.7 %collective-permute-start.9 = (bf16[4,64,128]{2,1,0:T(8,128)(2,1)S(1)}, bf16[4,64,128]{2,1,0:T(8,128)(2,1)S(1)}, u32[]{:S(2)}, u32[]{:S(2)}) collective-permute-start(bf16[4,64,128]{2,1,0:T(8,128)(2,1)S(1)} %get-tuple-element.81), channel_id=1, source_target_pairs={{0,8},{1,9},{2,10},{3,11},{4,12},{5,13},{6,14},{7,15},{16,24},{17,... | collective-permute-start | bytes 196616 | tf_op jit(solution)/shard_map/ppermute | solution.py:43
  42.9 3.6 %collective-permute-start.4 = (bf16[1,2048]{1,0:T(2,128)(2,1)S(1)}, bf16[1,2048]{1,0:T(2,128)(2,1)S(1)}, u32[]{:S(2)}, u32[]{:S(2)}) collective-permute-start(bf16[1,2048]{1,0:T(2,128)(2,1)S(1)} %convert_element_type.266), channel_id=1, source_target_pairs={{0,1},{1,2},{2,3},{3,4},{4,5},{5,6},{6,7},{7,8},{8,9},{9,10},{10,1... | collective-permute-start | bytes 12296 | tf_op jit(solution)/shard_map/ppermute | solution.py:22
  47.4 1.8 %collective-permute-start.6 = (f32[1,2,2048]{2,1,0:T(2,128)S(1)}, f32[1,2,2048]{2,1,0:T(2,128)S(1)}, u32[]{:S(2)}, u32[]{:S(2)}) collective-permute-start(f32[1,2,2048]{2,1,0:T(2,128)S(1)} %pad_maximum_fusion.12), channel_id=1, source_target_pairs={{0,1},{1,0},{2,3},{3,2},{4,5},{5,4},{6,7},{7,6},{8,9},{9,8},{10,11... | collective-permute-start | bytes 49160 | tf_op jit(solution)/shard_map/ppermute | solution.py:33
  54.2 2.4 %collective-permute-start.7 = (f32[2,2,2048]{2,1,0:T(2,128)S(1)}, f32[2,2,2048]{2,1,0:T(2,128)S(1)}, u32[]{:S(2)}, u32[]{:S(2)}) collective-permute-start(f32[2,2,2048]{2,1,0:T(2,128)S(1)} %maximum_select_fusion.2), channel_id=1, source_target_pairs={{0,2},{1,3},{2,0},{3,1},{4,6},{5,7},{6,4},{7,5},{8,10},{9,11},{10,... | collective-permute-start | bytes 98312 | tf_op jit(solution)/shard_map/ppermute | solution.py:33
  60.1 2.2 %collective-permute-start.8 = (f32[4,2,2048]{2,1,0:T(2,128)S(1)}, f32[4,2,2048]{2,1,0:T(2,128)S(1)}, u32[]{:S(2)}, u32[]{:S(2)}) collective-permute-start(f32[4,2,2048]{2,1,0:T(2,128)S(1)} %maximum_select_fusion.1), channel_id=1, source_target_pairs={{0,4},{1,5},{2,6},{3,7},{4,0},{5,1},{6,2},{7,3},{8,12},{9,13},{10,... | collective-permute-start | bytes 196616 | tf_op jit(solution)/shard_map/ppermute | solution.py:33
  62.8 1.8 %collective-permute-done.8 = f32[4,2,2048]{2,1,0:T(2,128)S(1)} collective-permute-done((f32[4,2,2048]{2,1,0:T(2,128)S(1)}, f32[4,2,2048]{2,1,0:T(2,128)S(1)}, u32[]{:S(2)}, u32[]{:S(2)}) %collective-permute-start.8) | collective-permute-done | bytes 65568 | tf_op jit(solution)/shard_map/ppermute | solution.py:33
  72.2 1.7 fusion.155
  75.1 1.9 %copy.58 = f32[16,64,64,2]{1,0,3,2:T(8,128)} copy(f32[16,64,64,2]{2,0,1,3:T(8,128)S(1)} %get-tuple-element.64) | data formatting | bytes 1048576 | tf_op jit(solution)/shard_map/integer_pow | solution.py:182
  77.0 1.6 copy.59
  78.7 4.3 %fusion.164 = (f32[16,64,128]{2,1,0:T(8,128)S(1)}, f32[16,64,128]{2,1,0:T(8,128)}) fusion(f32[1,16,64,128]{3,2,1,0:T(8,128)} %param.22, f32[16,64,128]{2,1,0:T(8,128)S(1)} %copy.59, f32[1,16,64,128]{3,2,1,0:T(8,128)S(1)} %copy-done.2, f32[24,72,136]{2,1,0:T(8,128)S(1)} %select_maximum_fusion.6, f32[4,64,128]{2,1,0:T(8,128)} %copy-done.11, ...), kind=kLoop, calls=%fused_computation.321 | loop fusion | flops 5373952 | bytes 11796480 | tf_op jit(solution)/shard_map/add | solution.py:203
  85.8 5.2 %collective-permute-start.11 = (bf16[4,64,128]{2,1,0:T(8,128)(2,1)S(1)}, bf16[4,64,128]{2,1,0:T(8,128)(2,1)S(1)}, u32[]{:S(2)}, u32[]{:S(2)}) collective-permute-start(bf16[4,64,128]{2,1,0:T(8,128)(2,1)S(1)} %get-tuple-element.79), channel_id=1, source_target_pairs={{0,8},{1,9},{2,10},{3,11},{4,12},{5,13},{6,14},{7,15},{16,24},{17,... | collective-permute-start | bytes 196616 | tf_op jit(solution)/shard_map/ppermute | solution.py:43
  92.9 5.2 %collective-permute-done.12 = bf16[4,64,128]{2,1,0:T(8,128)(2,1)S(1)} collective-permute-done((bf16[4,64,128]{2,1,0:T(8,128)(2,1)S(1)}, bf16[4,64,128]{2,1,0:T(8,128)(2,1)S(1)}, u32[]{:S(2)}, u32[]{:S(2)}) %collective-permute-start.12) | collective-permute-done | bytes 65568 | tf_op jit(solution)/shard_map/ppermute | solution.py:43
  99.2 4.2 %multiply_add_fusion.2 = (f32[16,64,128]{2,1,0:T(8,128)S(1)}, f32[16,64,128]{2,1,0:T(8,128)}) fusion(f32[16,64,128]{2,1,0:T(8,128)} %copy-done.3, f32[16,64,128]{2,1,0:T(8,128)S(1)} %scatter-add.14, f32[1,16,64,128]{3,2,1,0:T(8,128)S(1)} %copy-done.2, f32[24,72,136]{2,1,0:T(8,128)S(1)} %select_maximum_fusion.4, f32[4,64,128]{2,1,0:T(8,128)} %copy-done.13, ...), kind=kLoop, calls=%fused_computation.326 | loop fusion | flops 5373952 | bytes 11272192 | tf_op jit(solution)/shard_map/add | solution.py:203
  106.3 1.6 collective-permute-start.13
  107.9 1.5 collective-permute-start.14
  111.7 3.3 %collective-permute-done.14 = bf16[4,64,128]{2,1,0:T(8,128)(2,1)S(1)} collective-permute-done((bf16[4,64,128]{2,1,0:T(8,128)(2,1)S(1)}, bf16[4,64,128]{2,1,0:T(8,128)(2,1)S(1)}, u32[]{:S(2)}, u32[]{:S(2)}) %collective-permute-start.14) | collective-permute-done | bytes 65568 | tf_op jit(solution)/shard_map/ppermute | solution.py:43
  116.2 4.2 %multiply_add_fusion.1 = (f32[16,64,128]{2,1,0:T(8,128)S(1)}, f32[16,64,128]{2,1,0:T(8,128)}) fusion(f32[16,64,128]{2,1,0:T(8,128)} %copy-done.3, f32[16,64,128]{2,1,0:T(8,128)S(1)} %scatter-add.14, f32[16,64,128]{2,1,0:T(8,128)S(1)} %scatter-add.15, f32[24,72,136]{2,1,0:T(8,128)S(1)} %select_maximum_fusion.2, f32[4,64,128]{2,1,0:T(8,128)} %copy-done.12, ...), kind=kLoop, calls=%fused_computation.325 | loop fusion | flops 5373952 | bytes 11272192 | tf_op jit(solution)/shard_map/add | solution.py:203
  123.2 2.2 %collective-permute-start.15 = (bf16[4,64,128]{2,1,0:T(8,128)(2,1)S(1)}, bf16[4,64,128]{2,1,0:T(8,128)(2,1)S(1)}, u32[]{:S(2)}, u32[]{:S(2)}) collective-permute-start(bf16[4,64,128]{2,1,0:T(8,128)(2,1)S(1)} %get-tuple-element.75), channel_id=1, source_target_pairs={{0,8},{1,9},{2,10},{3,11},{4,12},{5,13},{6,14},{7,15},{16,24},{17,... | collective-permute-start | bytes 196616 | tf_op jit(solution)/shard_map/ppermute | solution.py:43
  127.4 1.9 %copy.63 = f32[16,64,64,2]{1,0,3,2:T(8,128)} copy(f32[16,64,64,2]{2,0,1,3:T(8,128)S(1)} %copy-done.5) | data formatting | bytes 1048576 | tf_op jit(solution)/shard_map/mul | solution.py:216
  129.3 2.4 %copy.64 = f32[16,64,128]{2,1,0:T(8,128)} copy(f32[16,64,128]{1,0,2:T(8,128)} %bitcast.569) | data formatting | bytes 1048576 | tf_op jit(solution)/shard_map/mul | solution.py:216
  136.1 3.3 %fusion.158 = (f32[16,64,128]{2,1,0:T(8,128)}, f32[16,64,128]{2,1,0:T(8,128)S(1)}) fusion(f32[16,64,128]{2,1,0:T(8,128)S(1)} %copy-done.10, f32[16,64,128]{2,1,0:T(8,128)S(1)} %copy-done.9, f32[16,64,128]{2,1,0:T(8,128)S(1)} %copy-done.8, f32[16,64,128]{2,1,0:T(8,128)S(1)} %copy-done.7, bf16[4,1,16,64,128]{4,3,2,1,0:T(8,128)(2,1)S(1)} %copy-done.14, ...), kind=kLoop, calls=%fused_computation.310 | loop fusion | flops 6422528 | bytes 13369344 | tf_op jit(solution)/shard_map/mul | solution.py:216
  143.9 1.5 copy.65
  148.7 5.4 %collective-permute-start.22 = (f32[1,2048]{1,0:T(1,128)S(1)}, f32[1,2048]{1,0:T(1,128)S(1)}, u32[]{:S(2)}, u32[]{:S(2)}) collective-permute-start(f32[1,2048]{1,0:T(1,128)S(1)} %get-tuple-element.91), channel_id=1, source_target_pairs={{0,8},{1,9},{2,10},{3,11},{4,12},{5,13},{6,14},{7,15},{16,24},{17,... | collective-permute-start | bytes 24584 | tf_op jit(solution)/shard_map/ppermute | solution.py:43
  155.6 5.0 %collective-permute-done.21 = f32[1,2048]{1,0:T(1,128)S(1)} collective-permute-done((f32[1,2048]{1,0:T(1,128)S(1)}, f32[1,2048]{1,0:T(1,128)S(1)}, u32[]{:S(2)}, u32[]{:S(2)}) %collective-permute-start.21) | collective-permute-done | bytes 8224 | tf_op jit(solution)/shard_map/ppermute | solution.py:43
  160.7 1.8 %collective-permute-start.18 = (f32[8,4,128]{2,1,0:T(4,128)S(1)}, f32[8,4,128]{2,1,0:T(4,128)S(1)}, u32[]{:S(2)}, u32[]{:S(2)}) collective-permute-start(f32[8,4,128]{2,1,0:T(4,128)S(1)} %fusion.474), channel_id=1, source_target_pairs={{0,2},{1,3},{2,0},{3,1},{4,6},{5,7},{6,4},{7,5},{8,10},{9,11},{10,... | collective-permute-start | bytes 49160 | tf_op jit(solution)/shard_map/ppermute | solution.py:215
  162.5 1.9 %collective-permute-start.23 = (f32[4,1,2048]{2,0,1:T(4,128)S(1)}, f32[4,1,2048]{2,0,1:T(4,128)S(1)}, u32[]{:S(2)}, u32[]{:S(2)}) collective-permute-start(f32[4,1,2048]{2,0,1:T(4,128)S(1)} %select_bitcast_fusion), channel_id=1, source_target_pairs={{0,4},{1,5},{2,6},{3,7},{4,0},{5,1},{6,2},{7,3},{8,12},{9,13},{10,... | collective-permute-start | bytes 98312 | tf_op jit(solution)/shard_map/ppermute | solution.py:33
  164.7 2.0 %collective-permute-start.19 = (f32[8,4,128]{2,1,0:T(4,128)S(1)}, f32[8,4,128]{2,1,0:T(4,128)S(1)}, u32[]{:S(2)}, u32[]{:S(2)}) collective-permute-start(f32[8,4,128]{2,1,0:T(4,128)S(1)} %fusion.500), channel_id=1, source_target_pairs={{0,4},{1,5},{2,6},{3,7},{4,0},{5,1},{6,2},{7,3},{8,12},{9,13},{10,... | collective-permute-start | bytes 49160 | tf_op jit(solution)/shard_map/ppermute | solution.py:215
  166.7 1.6 collective-permute-start.24
  168.5 2.0 %collective-permute-done.24 = f32[2,1,2048]{2,0,1:T(2,128)S(1)} collective-permute-done((f32[2,1,2048]{2,0,1:T(2,128)S(1)}, f32[2,1,2048]{2,0,1:T(2,128)S(1)}, u32[]{:S(2)}, u32[]{:S(2)}) %collective-permute-start.24) | collective-permute-done | bytes 16416 | tf_op jit(solution)/shard_map/ppermute | solution.py:33
  170.6 2.5 %collective-permute-done.20 = f32[8,4,128]{2,1,0:T(4,128)S(1)} collective-permute-done((f32[8,4,128]{2,1,0:T(4,128)S(1)}, f32[8,4,128]{2,1,0:T(4,128)S(1)}, u32[]{:S(2)}, u32[]{:S(2)}) %collective-permute-start.20) | collective-permute-done | bytes 16416 | tf_op jit(solution)/shard_map/ppermute | solution.py:215
  (266 shorter events, 59.3 us)
Async XLA Ops:
  0.6 32.1 %copy-start = (f32[8,4]{0,1:T(4,128)S(1)}, f32[8,4]{0,1:T(4,128)}, u32[]{:S(2)}) copy-start(f32[8,4]{0,1:T(4,128)} %param.25) | copy-start | bytes 388
  0.6 7.1 %copy-start.17 = (bf16[27,64,64]{2,1,0:T(8,128)(2,1)S(1)}, bf16[27,64,64]{2,1,0:T(8,128)(2,1)}, u32[]{:S(2)}) copy-start(bf16[27,64,64]{2,1,0:T(8,128)(2,1)} %param.19) | copy-start | bytes 663556
  0.7 5.6 %collective-permute-start.1 = (bf16[64,1,2048]{2,0,1:T(8,128)(2,1)}, bf16[64,1,2048]{2,0,1:T(8,128)(2,1)S(1)}, u32[]{:S(2)}, u32[]{:S(2)}) collective-permute-start(bf16[64,1,2048]{2,0,1:T(8,128)(2,1)} %param.18), channel_id=1, source_target_pairs={{1,0},{2,1},{3,2},{4,3},{5,4},{6,5},{7,6},{8,7},{9,8},{10,9},{11,1... | collective-permute-start | bytes 786440 | tf_op jit(solution)/shard_map/ppermute | solution.py:25
  2.1 4.4 %collective-permute-start = (bf16[64,1,2048]{2,0,1:T(8,128)(2,1)}, bf16[64,1,2048]{2,0,1:T(8,128)(2,1)S(1)}, u32[]{:S(2)}, u32[]{:S(2)}) collective-permute-start(bf16[64,1,2048]{2,0,1:T(8,128)(2,1)} %param.18), channel_id=1, source_target_pairs={{0,1},{1,2},{2,3},{3,4},{4,5},{5,6},{6,7},{7,8},{8,9},{9,10},{10,1... | collective-permute-start | bytes 786440 | tf_op jit(solution)/shard_map/ppermute | solution.py:22
  14.9 19.0 %copy-start.16 = (bf16[27,64,64]{2,1,0:T(8,128)(2,1)S(1)}, bf16[27,64,64]{2,1,0:T(8,128)(2,1)}, u32[]{:S(2)}) copy-start(bf16[27,64,64]{2,1,0:T(8,128)(2,1)} %param.20) | copy-start | bytes 663556
  15.2 18.2 %collective-permute-start.3 = (bf16[64,1,2048]{2,0,1:T(8,128)(2,1)S(1)}, bf16[64,1,2048]{2,0,1:T(8,128)(2,1)S(1)}, u32[]{:S(2)}, u32[]{:S(2)}) collective-permute-start(bf16[64,1,2048]{2,0,1:T(8,128)(2,1)S(1)} %bitcast.576), channel_id=1, source_target_pairs={{1,0},{2,1},{3,2},{4,3},{5,4},{6,5},{7,6},{8,7},{9,8},{10,9},{11,1... | collective-permute-start | bytes 786440 | tf_op jit(solution)/shard_map/ppermute | solution.py:25
  16.5 16.9 %collective-permute-start.2 = (bf16[64,1,2048]{2,0,1:T(8,128)(2,1)S(1)}, bf16[64,1,2048]{2,0,1:T(8,128)(2,1)S(1)}, u32[]{:S(2)}, u32[]{:S(2)}) collective-permute-start(bf16[64,1,2048]{2,0,1:T(8,128)(2,1)S(1)} %bitcast.577), channel_id=1, source_target_pairs={{0,1},{1,2},{2,3},{3,4},{4,5},{5,6},{6,7},{7,8},{8,9},{9,10},{10,1... | collective-permute-start | bytes 786440 | tf_op jit(solution)/shard_map/ppermute | solution.py:22
  25.7 34.3 %collective-permute-start.9 = (bf16[4,64,128]{2,1,0:T(8,128)(2,1)S(1)}, bf16[4,64,128]{2,1,0:T(8,128)(2,1)S(1)}, u32[]{:S(2)}, u32[]{:S(2)}) collective-permute-start(bf16[4,64,128]{2,1,0:T(8,128)(2,1)S(1)} %get-tuple-element.81), channel_id=1, source_target_pairs={{0,8},{1,9},{2,10},{3,11},{4,12},{5,13},{6,14},{7,15},{16,24},{17,... | collective-permute-start | bytes 196616 | tf_op jit(solution)/shard_map/ppermute | solution.py:43
  31.4 28.6 %collective-permute-start.10 = (bf16[4,64,128]{2,1,0:T(8,128)(2,1)S(1)}, bf16[4,64,128]{2,1,0:T(8,128)(2,1)S(1)}, u32[]{:S(2)}, u32[]{:S(2)}) collective-permute-start(bf16[4,64,128]{2,1,0:T(8,128)(2,1)S(1)} %get-tuple-element.82), channel_id=1, source_target_pairs={{8,0},{9,1},{10,2},{11,3},{12,4},{13,5},{14,6},{15,7},{24,16},{25,... | collective-permute-start | bytes 196616 | tf_op jit(solution)/shard_map/ppermute | solution.py:43
  40.7 16.0 %copy-start.21 = (s32[3]{0:T(128)S(1)}, s32[3]{0:T(128)}, u32[]{:S(2)}) copy-start(s32[3]{0:T(128)} %constant.246.clone.1) | copy-start | bytes 40
  40.7 21.6 %copy-start.2 = (f32[1,16,64,128]{3,2,1,0:T(8,128)S(1)}, f32[1,16,64,128]{3,2,1,0:T(8,128)}, u32[]{:S(2)}) copy-start(f32[1,16,64,128]{3,2,1,0:T(8,128)} %param.23) | copy-start | bytes 1572868
  41.6 5.0 %collective-permute-start.5 = (bf16[1,2048]{1,0:T(2,128)(2,1)S(1)}, bf16[1,2048]{1,0:T(2,128)(2,1)S(1)}, u32[]{:S(2)}, u32[]{:S(2)}) collective-permute-start(bf16[1,2048]{1,0:T(2,128)(2,1)S(1)} %convert_element_type.266), channel_id=1, source_target_pairs={{1,0},{2,1},{3,2},{4,3},{5,4},{6,5},{7,6},{8,7},{9,8},{10,9},{11,1... | collective-permute-start | bytes 12296 | tf_op jit(solution)/shard_map/ppermute | solution.py:25
  42.9 4.3 %collective-permute-start.4 = (bf16[1,2048]{1,0:T(2,128)(2,1)S(1)}, bf16[1,2048]{1,0:T(2,128)(2,1)S(1)}, u32[]{:S(2)}, u32[]{:S(2)}) collective-permute-start(bf16[1,2048]{1,0:T(2,128)(2,1)S(1)} %convert_element_type.266), channel_id=1, source_target_pairs={{0,1},{1,2},{2,3},{3,4},{4,5},{5,6},{6,7},{7,8},{8,9},{9,10},{10,1... | collective-permute-start | bytes 12296 | tf_op jit(solution)/shard_map/ppermute | solution.py:22
  47.4 6.8 %collective-permute-start.6 = (f32[1,2,2048]{2,1,0:T(2,128)S(1)}, f32[1,2,2048]{2,1,0:T(2,128)S(1)}, u32[]{:S(2)}, u32[]{:S(2)}) collective-permute-start(f32[1,2,2048]{2,1,0:T(2,128)S(1)} %pad_maximum_fusion.12), channel_id=1, source_target_pairs={{0,1},{1,0},{2,3},{3,2},{4,5},{5,4},{6,7},{7,6},{8,9},{9,8},{10,11... | collective-permute-start | bytes 49160 | tf_op jit(solution)/shard_map/ppermute | solution.py:33
  54.2 5.8 %collective-permute-start.7 = (f32[2,2,2048]{2,1,0:T(2,128)S(1)}, f32[2,2,2048]{2,1,0:T(2,128)S(1)}, u32[]{:S(2)}, u32[]{:S(2)}) collective-permute-start(f32[2,2,2048]{2,1,0:T(2,128)S(1)} %maximum_select_fusion.2), channel_id=1, source_target_pairs={{0,2},{1,3},{2,0},{3,1},{4,6},{5,7},{6,4},{7,5},{8,10},{9,11},{10,... | collective-permute-start | bytes 98312 | tf_op jit(solution)/shard_map/ppermute | solution.py:33
  60.1 4.5 %collective-permute-start.8 = (f32[4,2,2048]{2,1,0:T(2,128)S(1)}, f32[4,2,2048]{2,1,0:T(2,128)S(1)}, u32[]{:S(2)}, u32[]{:S(2)}) collective-permute-start(f32[4,2,2048]{2,1,0:T(2,128)S(1)} %maximum_select_fusion.1), channel_id=1, source_target_pairs={{0,4},{1,5},{2,6},{3,7},{4,0},{5,1},{6,2},{7,3},{8,12},{9,13},{10,... | collective-permute-start | bytes 196616 | tf_op jit(solution)/shard_map/ppermute | solution.py:33
  85.8 7.1 %collective-permute-start.11 = (bf16[4,64,128]{2,1,0:T(8,128)(2,1)S(1)}, bf16[4,64,128]{2,1,0:T(8,128)(2,1)S(1)}, u32[]{:S(2)}, u32[]{:S(2)}) collective-permute-start(bf16[4,64,128]{2,1,0:T(8,128)(2,1)S(1)} %get-tuple-element.79), channel_id=1, source_target_pairs={{0,8},{1,9},{2,10},{3,11},{4,12},{5,13},{6,14},{7,15},{16,24},{17,... | collective-permute-start | bytes 196616 | tf_op jit(solution)/shard_map/ppermute | solution.py:43
  91.0 7.1 %collective-permute-start.12 = (bf16[4,64,128]{2,1,0:T(8,128)(2,1)S(1)}, bf16[4,64,128]{2,1,0:T(8,128)(2,1)S(1)}, u32[]{:S(2)}, u32[]{:S(2)}) collective-permute-start(bf16[4,64,128]{2,1,0:T(8,128)(2,1)S(1)} %get-tuple-element.80), channel_id=1, source_target_pairs={{8,0},{9,1},{10,2},{11,3},{12,4},{13,5},{14,6},{15,7},{24,16},{25,... | collective-permute-start | bytes 196616 | tf_op jit(solution)/shard_map/ppermute | solution.py:43
  106.3 5.3 %collective-permute-start.13 = (bf16[4,64,128]{2,1,0:T(8,128)(2,1)S(1)}, bf16[4,64,128]{2,1,0:T(8,128)(2,1)S(1)}, u32[]{:S(2)}, u32[]{:S(2)}) collective-permute-start(bf16[4,64,128]{2,1,0:T(8,128)(2,1)S(1)} %get-tuple-element.77), channel_id=1, source_target_pairs={{0,8},{1,9},{2,10},{3,11},{4,12},{5,13},{6,14},{7,15},{16,24},{17,... | collective-permute-start | bytes 196616 | tf_op jit(solution)/shard_map/ppermute | solution.py:43
  107.9 7.1 %collective-permute-start.14 = (bf16[4,64,128]{2,1,0:T(8,128)(2,1)S(1)}, bf16[4,64,128]{2,1,0:T(8,128)(2,1)S(1)}, u32[]{:S(2)}, u32[]{:S(2)}) collective-permute-start(bf16[4,64,128]{2,1,0:T(8,128)(2,1)S(1)} %get-tuple-element.78), channel_id=1, source_target_pairs={{8,0},{9,1},{10,2},{11,3},{12,4},{13,5},{14,6},{15,7},{24,16},{25,... | collective-permute-start | bytes 196616 | tf_op jit(solution)/shard_map/ppermute | solution.py:43
  123.2 11.6 %collective-permute-start.15 = (bf16[4,64,128]{2,1,0:T(8,128)(2,1)S(1)}, bf16[4,64,128]{2,1,0:T(8,128)(2,1)S(1)}, u32[]{:S(2)}, u32[]{:S(2)}) collective-permute-start(bf16[4,64,128]{2,1,0:T(8,128)(2,1)S(1)} %get-tuple-element.75), channel_id=1, source_target_pairs={{0,8},{1,9},{2,10},{3,11},{4,12},{5,13},{6,14},{7,15},{16,24},{17,... | collective-permute-start | bytes 196616 | tf_op jit(solution)/shard_map/ppermute | solution.py:43
  125.4 9.4 %collective-permute-start.16 = (bf16[4,64,128]{2,1,0:T(8,128)(2,1)S(1)}, bf16[4,64,128]{2,1,0:T(8,128)(2,1)S(1)}, u32[]{:S(2)}, u32[]{:S(2)}) collective-permute-start(bf16[4,64,128]{2,1,0:T(8,128)(2,1)S(1)} %get-tuple-element.76), channel_id=1, source_target_pairs={{8,0},{9,1},{10,2},{11,3},{12,4},{13,5},{14,6},{15,7},{24,16},{25,... | collective-permute-start | bytes 196616 | tf_op jit(solution)/shard_map/ppermute | solution.py:43
  147.6 26.7 %copy-start.1 = (f32[8,4]{0,1:T(4,128)S(1)}, f32[8,4]{0,1:T(4,128)}, u32[]{:S(2)}) copy-start(f32[8,4]{0,1:T(4,128)} %param.25) | copy-start | bytes 388
  148.7 6.9 %collective-permute-start.22 = (f32[1,2048]{1,0:T(1,128)S(1)}, f32[1,2048]{1,0:T(1,128)S(1)}, u32[]{:S(2)}, u32[]{:S(2)}) collective-permute-start(f32[1,2048]{1,0:T(1,128)S(1)} %get-tuple-element.91), channel_id=1, source_target_pairs={{0,8},{1,9},{2,10},{3,11},{4,12},{5,13},{6,14},{7,15},{16,24},{17,... | collective-permute-start | bytes 24584 | tf_op jit(solution)/shard_map/ppermute | solution.py:43
  154.1 6.4 %collective-permute-start.21 = (f32[1,2048]{1,0:T(1,128)S(1)}, f32[1,2048]{1,0:T(1,128)S(1)}, u32[]{:S(2)}, u32[]{:S(2)}) collective-permute-start(f32[1,2048]{1,0:T(1,128)S(1)} %get-tuple-element.92), channel_id=1, source_target_pairs={{8,0},{9,1},{10,2},{11,3},{12,4},{13,5},{14,6},{15,7},{24,16},{25,... | collective-permute-start | bytes 24584 | tf_op jit(solution)/shard_map/ppermute | solution.py:43
  155.5 5.1 %collective-permute-start.17 = (f32[8,4,128]{2,1,0:T(4,128)S(1)}, f32[8,4,128]{2,1,0:T(4,128)S(1)}, u32[]{:S(2)}, u32[]{:S(2)}) collective-permute-start(f32[8,4,128]{2,1,0:T(4,128)S(1)} %broadcast_select_fusion.9), channel_id=1, source_target_pairs={{0,1},{1,0},{2,3},{3,2},{4,5},{5,4},{6,7},{7,6},{8,9},{9,8},{10,11... | collective-permute-start | bytes 49160 | tf_op jit(solution)/shard_map/ppermute | solution.py:215
  160.7 3.9 %collective-permute-start.18 = (f32[8,4,128]{2,1,0:T(4,128)S(1)}, f32[8,4,128]{2,1,0:T(4,128)S(1)}, u32[]{:S(2)}, u32[]{:S(2)}) collective-permute-start(f32[8,4,128]{2,1,0:T(4,128)S(1)} %fusion.474), channel_id=1, source_target_pairs={{0,2},{1,3},{2,0},{3,1},{4,6},{5,7},{6,4},{7,5},{8,10},{9,11},{10,... | collective-permute-start | bytes 49160 | tf_op jit(solution)/shard_map/ppermute | solution.py:215
  162.5 4.1 %collective-permute-start.23 = (f32[4,1,2048]{2,0,1:T(4,128)S(1)}, f32[4,1,2048]{2,0,1:T(4,128)S(1)}, u32[]{:S(2)}, u32[]{:S(2)}) collective-permute-start(f32[4,1,2048]{2,0,1:T(4,128)S(1)} %select_bitcast_fusion), channel_id=1, source_target_pairs={{0,4},{1,5},{2,6},{3,7},{4,0},{5,1},{6,2},{7,3},{8,12},{9,13},{10,... | collective-permute-start | bytes 98312 | tf_op jit(solution)/shard_map/ppermute | solution.py:33
  164.7 3.8 %collective-permute-start.19 = (f32[8,4,128]{2,1,0:T(4,128)S(1)}, f32[8,4,128]{2,1,0:T(4,128)S(1)}, u32[]{:S(2)}, u32[]{:S(2)}) collective-permute-start(f32[8,4,128]{2,1,0:T(4,128)S(1)} %fusion.500), channel_id=1, source_target_pairs={{0,4},{1,5},{2,6},{3,7},{4,0},{5,1},{6,2},{7,3},{8,12},{9,13},{10,... | collective-permute-start | bytes 49160 | tf_op jit(solution)/shard_map/ppermute | solution.py:215
  166.7 3.8 %collective-permute-start.24 = (f32[2,1,2048]{2,0,1:T(2,128)S(1)}, f32[2,1,2048]{2,0,1:T(2,128)S(1)}, u32[]{:S(2)}, u32[]{:S(2)}) collective-permute-start(f32[2,1,2048]{2,0,1:T(2,128)S(1)} %broadcast_select_fusion.4), channel_id=1, source_target_pairs={{0,2},{1,3},{2,0},{3,1},{4,6},{5,7},{6,4},{7,5},{8,10},{9,11},{10,... | collective-permute-start | bytes 49160 | tf_op jit(solution)/shard_map/ppermute | solution.py:33
  168.5 4.6 %collective-permute-start.20 = (f32[8,4,128]{2,1,0:T(4,128)S(1)}, f32[8,4,128]{2,1,0:T(4,128)S(1)}, u32[]{:S(2)}, u32[]{:S(2)}) collective-permute-start(f32[8,4,128]{2,1,0:T(4,128)S(1)} %add.1218), channel_id=1, source_target_pairs={{0,8},{1,9},{2,10},{3,11},{4,12},{5,13},{6,14},{7,15},{8,0},{9,1},... | collective-permute-start | bytes 49160 | tf_op jit(solution)/shard_map/ppermute | solution.py:215
  170.5 3.2 %collective-permute-start.25 = (f32[1,1,2048]{2,0,1:T(1,128)S(1)}, f32[1,1,2048]{2,0,1:T(1,128)S(1)}, u32[]{:S(2)}, u32[]{:S(2)}) collective-permute-start(f32[1,1,2048]{2,0,1:T(1,128)S(1)} %broadcast_select_fusion.5), channel_id=1, source_target_pairs={{0,1},{1,0},{2,3},{3,2},{4,5},{5,4},{6,7},{7,6},{8,9},{9,8},{10,11... | collective-permute-start | bytes 24584 | tf_op jit(solution)/shard_map/ppermute | solution.py:33
  (17 other events, 42.3 us)
